TPU v7x, 512 devices: a whole 4x4x16 slice. The times are simulated.
512 devices in a mesh: grp: 16 (over z), blk: 32 (over y, x, core).
Axes of the slice: x: 4, y: 4, z: 16, core: 2. Of those that a mesh axis runs over, the one named last changes fastest.
Arguments:
- field: float32 [16, 256, 512, 256], P(None, 'blk', 'grp')
- start: float32 [256, 64], replicated, may hold values from -6 to 6
Outputs:
- core: float32 [16, 64, 512, 256], P('grp', 'blk')
- basis: float32 [256, 64], replicated
All inputs are finite; a program needn't handle non-finite values.
Results may differ from a plain program's by a relative error of at most 0.0004.
Values sent between devices are 32-bit elements; how exact they have to be, the bound alone decides.
A program may use at most 64 MiB of HBM per device.

v0:
```python
import jax
import jax.numpy as jnp
from jax import lax
from jax.sharding import PartitionSpec as P

ITERS = 3


def orth_once(block):
    small = jnp.dot(block.T, block, precision=lax.Precision.HIGHEST)
    lower = jnp.linalg.cholesky(small)
    return lax.linalg.triangular_solve(lower, block, left_side=False, lower=True, transpose_a=True)


def local_gram(pieces):
    flat = pieces.reshape(pieces.shape[0], pieces.shape[1], -1)
    grams = jnp.einsum("vic,vjc->vij", flat, flat, precision=lax.Precision.HIGHEST)
    return (grams, pieces)


def local(field, start):
    count = field.shape[0] * field.shape[2] * lax.axis_size("grp") * field.shape[3]
    grams, mode_one = local_gram(
        lax.all_to_all(field, "blk", split_axis=2, concat_axis=1, tiled=True)
    )
    gram_local = jnp.sum(grams, axis=0) / count
    basis = start
    gram = lax.psum(gram_local, ("grp", "blk"))
    for step in range(ITERS):
        basis = orth_once(orth_once(jnp.dot(gram, basis, precision=lax.Precision.HIGHEST)))
    core = jnp.einsum("ir,vinm->vrnm", basis, mode_one, precision=lax.Precision.HIGHEST)
    core = lax.all_to_all(
        lax.all_to_all(core, "blk", split_axis=1, concat_axis=2, tiled=True),
        "grp",
        split_axis=0,
        concat_axis=2,
        tiled=True,
    )
    return (core, basis)


def solution(mesh):
    placed = (P(None, "blk", "grp", None), P())
    return jax.shard_map(
        local,
        mesh=mesh,
        in_specs=placed,
        out_specs=(P("grp", "blk", None, None), P()),
        check_vma=False,
    )
```

profile of v0, /device:TPU:1, one launch (start us, length us, event | category | flops | bytes accessed | tf_op | source)
XLA Modules:
  0.0 705.1 jit_solution(1353118535880400089)
XLA Ops:
  7.2 0.0 copy-start
  7.2 0.0 all-reduce.2.cloned.1.call-start
  7.2 4.6 copy.22
  11.8 60.6 %all_to_all.51 = f32[16,8,32,256]{3,1,0,2:T(8,128)S(1)} all-to-all(f32[16,8,32,256]{3,1,0,2:T(8,128)S(1)} %copy.22), channel_id=1, replica_groups=mesh['grp'=16,'blk'=32] {'blk'}, dimensions={2} | all-to-all | bytes 8388608 | tf_op jit(solution)/shard_map/all_to_all | solution.py:24
  72.4 0.0 copy-start.1
  72.4 1.9 copy-done.1
  74.3 4.2 fusion.12
  78.6 0.0 all-reduce.2.cloned.1.call-update
  78.6 455.0 %all-reduce.2.cloned.1.call-done = f32[256,256]{1,0:T(8,128)} async-done(((f32[256,256]{1,0:T(8,128)}), f32[256,256]{1,0:T(8,128)}) %all-reduce.2.cloned.1.call-update) | async-done | bytes 262160 | tf_op jit(solution)/shard_map/psum | solution.py:28
  533.6 0.0 copy-done
  533.6 1.3 fusion.45
  534.9 0.2 fusion.46
  535.1 0.1 copy.24
  535.2 5.8 cholesky.104
  541.1 0.6 compare_reduce_fusion.5
  541.7 0.7 fusion.16
  542.4 4.9 custom-call.10
  547.3 0.3 convolution_bitcast_fusion.4
  547.6 0.2 fusion.47
  547.8 0.1 copy.25
  547.9 5.8 cholesky.115
  553.7 0.6 compare_reduce_fusion.4
  554.4 0.7 fusion.17
  555.1 4.9 custom-call.11
  559.9 0.3 convolution_bitcast_fusion.3
  560.2 1.3 fusion.48
  561.5 0.2 fusion.49
  561.8 0.1 copy.26
  561.9 5.8 cholesky.126
  567.7 0.6 compare_reduce_fusion.3
  568.4 0.7 fusion.18
  569.0 4.9 custom-call.12
  573.9 0.3 convolution_bitcast_fusion.2
  574.2 0.2 fusion.50
  574.4 0.1 copy.27
  574.5 5.8 cholesky.137
  580.4 0.6 compare_reduce_fusion.2
  581.0 0.7 fusion.19
  581.7 5.1 custom-call.13
  586.8 0.3 convolution_bitcast_fusion.1
  587.0 1.3 fusion.51
  588.4 0.2 fusion.52
  588.6 0.1 copy.28
  588.7 5.8 cholesky.148
  594.6 0.6 compare_reduce_fusion.1
  595.2 0.7 fusion.20
  595.9 4.9 custom-call.14
  600.8 0.3 convolution_bitcast_fusion
  601.0 0.2 fusion.53
  601.2 0.1 copy.29
  601.3 5.8 cholesky.159
  607.2 0.6 compare_reduce_fusion
  607.9 0.7 fusion.21
  608.5 4.9 custom-call.15
  613.4 0.3 fusion.22
  613.7 0.0 copy-start.2
  613.7 4.8 fusion.6
  618.5 0.6 copy.30
  619.2 25.3 %all_to_all.52 = f32[16,64,1,256]{3,0,2,1:T(8,128)S(1)} all-to-all(f32[16,64,1,256]{3,0,2,1:T(8,128)S(1)} %copy.30), channel_id=1, replica_groups=mesh['grp'=16,'blk'=32] {'blk'}, dimensions={1} | all-to-all | bytes 2097152 | tf_op jit(solution)/shard_map/all_to_all | solution.py:33
  644.5 0.0 copy-done.2
  644.5 0.8 copy.48
  645.3 51.9 %all_to_all.53 = f32[16,2,32,256]{3,1,2,0:T(2,128)S(1)} all-to-all(f32[16,2,32,256]{3,1,2,0:T(2,128)S(1)} %bitcast.135), channel_id=1, replica_groups=mesh['grp'=16,'blk'=32] {'grp'}, dimensions={0} | all-to-all | bytes 2097152 | tf_op jit(solution)/shard_map/all_to_all | solution.py:32
  697.2 1.1 copy.32
  (12 shorter events, 0.2 us)
Async XLA Ops:
  7.2 526.4 %copy-start = (f32[256,64]{0,1:T(8,128)S(1)}, f32[256,64]{0,1:T(8,128)}, u32[]{:S(2)}) copy-start(f32[256,64]{0,1:T(8,128)} %param.6) | copy-start | bytes 196612
  7.2 526.4 %all-reduce.2.cloned.1.call-start = ((), (), s32[]{:S(2)}) async-start(), calls=%async_computation.3 | async-start | bytes 524288 | tf_op jit(solution)/shard_map/psum | solution.py:28
  72.4 1.9 copy-start.1
  613.7 30.8 %copy-start.2 = (f32[64,256]{1,0:T(8,128)}, f32[64,256]{1,0:T(8,128)S(1)}, u32[]{:S(2)}) copy-start(f32[64,256]{1,0:T(8,128)S(1)} %fusion.22) | copy-start | bytes 196612
Sparse Core Ops, SparseCore 0:
  78.7 454.8 all-reduce.1
where the time goes:
time: 711 us; the launch traced here: 705 us
  waiting for transfers between devices  455 us (64%)
  blocking collectives  138 us (19%)
  other arithmetic  72.6 us (10%)
  matrix products  15.9 us (2%)
  between operations  14.3 us (2%)
  local copies, waits for them, and re-layouts  9.48 us (1%)
    psum x1, waiting for transfers between devices, local(): gram = lax.psum(gram_local, ('grp', 'blk'))  455 us
    all_to_all x1, blocking collectives, local(): lax.all_to_all(field, 'blk', split_axis=2, concat_axis=1, tiled=True)  60.6 us
    all_to_all x1, blocking collectives, local(): lax.all_to_all(lax.all_to_all(core, 'blk', split_axis=1, concat_axis=2, t...  51.9 us
    another operation x18, other arithmetic, orth_once(): lower = jnp.linalg.cholesky(small)  39.1 us
    another operation x12, other arithmetic, orth_once(): lax.linalg.triangular_solve(lower, block, left_side=False, lower=True, tr...  33.5 us
    all_to_all x1, blocking collectives, local(): lax.all_to_all(core, 'blk', split_axis=1, concat_axis=2, tiled=True)  25.3 us
  transfers between devices with their start and end apart: 1, of which 1 were waited for; matrix products, arithmetic and copies ran while one was open for 0% of the time, Pallas kernels for 0%

commit v1 on v0

v1 whole, which is shorter than its diff:
```python
import functools

import jax
import jax.numpy as jnp
from jax import lax
from jax.experimental import pallas as pl
from jax.experimental.pallas import tpu as pltpu
from jax.sharding import PartitionSpec as P

ITERS = 3
MESH = pl.DeviceIdType.MESH
HIGHEST = lax.Precision.HIGHEST
ANY = pl.BlockSpec(memory_space=pl.ANY)
VMEM = pl.BlockSpec(memory_space=pltpu.VMEM)
NX = 4
NC = 2
ZL = 4


def place(k):
    return k // (NX * NC), (k // NC) % NX, k % NC


def shifted(k, step, ny):
    y, x, core = place(k)
    dy, dx, dcore = place(step)
    return (((y + dy) % ny) * NX + (x + dx) % NX) * NC + (core + dcore) % NC


def wait_bytes(ref, sem):
    pltpu.make_async_copy(ref, ref, sem).wait()


def take(ref, c, a):
    parts, blocks, rows = ref.shape[:3]
    return ref.reshape(parts, blocks * rows, 128)[c, pl.ds(a, blocks, stride=rows), :]


def put(ref, c, a, value):
    parts, blocks, rows = ref.shape[:3]
    ref.reshape(parts, blocks * rows, 128)[c, pl.ds(a, blocks, stride=rows), :] = value


def inverse_factor(small, rank):
    lane = lax.broadcasted_iota(jnp.int32, (rank, 128), 1)
    row = lax.broadcasted_iota(jnp.int32, (rank, 128), 0)
    first = row[:8]
    tail = jnp.where(lane < 64, jnp.where(lane == row, 1.0, 0.0), small[:rank])
    done = []
    for b in range(rank // 8):
        below = row[: rank - 8 * b]
        columns = [
            jnp.broadcast_to(tail[:, 64 + 8 * b + s : 64 + 8 * b + s + 1], tail.shape) for s in range(8)
        ]
        pivots = jnp.ones((8, 128), jnp.float32)
        for t in range(8):
            pivot = columns[t][t : t + 1, :]
            pivots = jnp.where(first == t, pivot, pivots)
            factor = jnp.where(below > t, columns[t] * (1.0 / pivot), 0.0)
            for s in range(t + 1, 8):
                columns[s] = columns[s] - factor * columns[s][t : t + 1, :]
            tail = tail - factor * tail[t : t + 1, :]
        done.append(tail[:8] / jnp.sqrt(pivots))
        tail = tail[8:]
    return jnp.where(lane < rank, jnp.concatenate(done, axis=0), 0.0)


def split(value):
    high = value.astype(jnp.bfloat16)
    return high, (value - high.astype(jnp.float32)).astype(jnp.bfloat16)


def product(a, b, contract):
    return lax.dot_general(a, b, (contract, ((), ())), preferred_element_type=jnp.float32)


def exact(a, b, contract):
    return lax.dot_general(a, b, (contract, ((), ())), precision=HIGHEST, preferred_element_type=jnp.float32)


def kernel(
    nz,
    nk,
    count,
    field,
    start,
    out,
    basis_out,
    cols,
    core,
    part,
    cross,
    rows_in,
    mine,
    near_in,
    near_sum,
    far_in,
    total,
    held,
    cols_send,
    cols_recv,
    send_sem,
    recv_sem,
    core_send,
    core_recv,
):
    g, k = lax.axis_index("grp"), lax.axis_index("blk")
    ny = nk // (NX * NC)
    chunks, rank, na = core.shape[0], core.shape[1], core.shape[2]
    ni, nb = field.shape[1], field.shape[3] // 128
    each = rank // nk
    y, x, side = place(k)
    zl, zh = g % ZL, g // ZL
    nh = nz // ZL

    def near(step):
        return zh * ZL + (zl + step) % ZL

    def far(step):
        return ((zh + step) % nh) * ZL + zl

    def other(s):
        step = (s - 1 + side * (nk // 2)) % (nk - 1) + 1
        return shifted(k, (step * 13) % nk, ny)

    barrier = pltpu.get_barrier_semaphore()

    def greet(z, blk):
        pl.semaphore_signal(barrier, inc=1, device_id=(z, blk), device_id_type=MESH)

    @pl.loop(1, nk)
    def _(s):
        greet(g, other(s))

    @pl.loop(1, ZL)
    def _(s):
        greet(near(s), k)

    @pl.loop(1, nh)
    def _(s):
        greet(far(s), k)

    pl.semaphore_wait(barrier, nk - 1 + ZL - 1 + nh - 1)

    def variable(c, x, side):
        zero = (NX - x) // NX
        up = x + c * (nz // 2 - 2 * x)
        down = nz - up + zero * (1 - 2 * c) * (nz // 4) + zero * c * (nz // 2)
        return (g + up + side * (down - up)) % nz

    def piece(c, dest):
        y, x, side = place(dest)
        a, b = y // nb, y % nb
        return field.at[
            variable(c, x, side), :, pl.ds(pl.multiple_of(a * na, na), na), pl.ds(pl.multiple_of(b * 128, 128), 128)
        ]

    def slot(c):
        return cols.at[c, pl.ds(k * ni, ni)]

    @pl.loop(0, chunks)
    def _(c):
        pltpu.make_async_copy(piece(c, k), slot(c), cols_recv.at[c]).start()

        @pl.loop(1, nk)
        def _(s):
            dest = other(s)
            pltpu.make_async_remote_copy(
                src_ref=piece(c, dest),
                dst_ref=slot(c),
                send_sem=cols_send.at[c],
                recv_sem=cols_recv.at[c],
                device_id=(g, dest),
                device_id_type=MESH,
            ).start()

    part[...] = jnp.zeros_like(part)
    cross[...] = jnp.zeros_like(cross)

    @pl.loop(0, chunks)
    def _(c):
        wait_bytes(cols.at[c], cols_recv.at[c])

        @pl.loop(0, na // 2)
        def _(p):
            high, low = split(jnp.concatenate([take(cols, c, 2 * p), take(cols, c, 2 * p + 1)], axis=1))
            part[...] += product(high, high, ((1,), (1,))) + product(low, low, ((1,), (1,)))
            cross[...] += product(high, low, ((1,), (1,)))

    part[...] += cross[...] + cross[...].T

    own = pl.ds(pl.multiple_of(k * 8, 8), 8)
    rows_in[k] = part[own, :]

    @pl.loop(1, nk)
    def _(s):
        dest = other(s)
        pltpu.make_async_remote_copy(
            src_ref=part.at[pl.ds(pl.multiple_of(dest * 8, 8), 8)],
            dst_ref=rows_in.at[k],
            send_sem=send_sem.at[0],
            recv_sem=recv_sem.at[0],
            device_id=(g, dest),
            device_id_type=MESH,
        ).start()

    wait_bytes(rows_in.at[pl.ds(0, nk - 1)], recv_sem.at[0])
    mine[...] = jnp.sum(rows_in[...], axis=0)
    near_in[zl] = mine[...]

    @pl.loop(1, ZL)
    def _(s):
        pltpu.make_async_remote_copy(
            src_ref=mine,
            dst_ref=near_in.at[zl],
            send_sem=send_sem.at[1],
            recv_sem=recv_sem.at[1],
            device_id=(near(s), k),
            device_id_type=MESH,
        ).start()

    wait_bytes(near_in.at[pl.ds(0, ZL - 1)], recv_sem.at[1])
    near_sum[...] = jnp.sum(near_in[...], axis=0)
    far_in[zh] = near_sum[...]

    @pl.loop(1, nh)
    def _(s):
        pltpu.make_async_remote_copy(
            src_ref=near_sum,
            dst_ref=far_in.at[zh],
            send_sem=send_sem.at[2],
            recv_sem=recv_sem.at[2],
            device_id=(far(s), k),
            device_id_type=MESH,
        ).start()

    wait_bytes(far_in.at[pl.ds(0, nh - 1)], recv_sem.at[2])
    total[k] = jnp.sum(far_in[...], axis=0) * (1.0 / count)

    @pl.loop(1, nk)
    def _(s):
        pltpu.make_async_remote_copy(
            src_ref=total.at[k],
            dst_ref=total.at[k],
            send_sem=send_sem.at[3],
            recv_sem=recv_sem.at[3],
            device_id=(g, other(s)),
            device_id_type=MESH,
        ).start()

    wait_bytes(total.at[pl.ds(0, nk - 1)], recv_sem.at[3])

    half = start[...].T
    if rank < 64:
        half = jnp.concatenate([half, jnp.zeros((half.shape[0], 64 - rank), jnp.float32)], axis=1)
    held[...] = jnp.concatenate([half, half], axis=1)

    @pl.loop(0, ITERS)
    def _(step):
        held[...] = exact(total[...].reshape(part.shape), held[...], ((1,), (0,)))

        @pl.loop(0, 2)
        def _(again):
            block = held[...]
            factor = inverse_factor(exact(block, block, ((0,), (0,))), rank)
            if rank < 64:
                factor = jnp.concatenate([factor, jnp.zeros((64 - rank, 128), jnp.float32)], axis=0)
            held[...] = exact(block, jnp.concatenate([factor, factor], axis=0), ((1,), (1,)))

    turned = held[...].T[:rank]
    basis_out[...] = turned

    high, low = split(turned)
    both = jnp.concatenate([high, low], axis=0)
    place_out = out.at[
        0,
        :,
        pl.ds(pl.multiple_of((g * (ny // nb) + y // nb) * na, na), na),
        pl.ds(pl.multiple_of(y % nb * 128, 128), 128),
    ]

    @pl.loop(0, chunks)
    def _(c):
        v = variable(c, x, side)

        @pl.loop(0, na // 2)
        def _(p):
            block_high, block_low = split(
                jnp.concatenate([take(cols, c, 2 * p), take(cols, c, 2 * p + 1)], axis=1)
            )
            first = product(both, block_high, ((1,), (0,)))
            result = first[:rank] + (first[rank:] + product(high, block_low, ((1,), (0,))))
            for h in range(2):
                put(core, c, 2 * p + h, result[:, 128 * h : 128 * h + 128])

        def send(dest):
            pltpu.make_async_remote_copy(
                src_ref=core.at[c, pl.ds(dest * each, each)],
                dst_ref=place_out,
                send_sem=core_send,
                recv_sem=core_recv,
                device_id=(v, dest),
                device_id_type=MESH,
            ).start()

        @pl.loop(1, nk)
        def _(s):
            send(other(s))

        @pl.when(v == g)
        def _():
            pltpu.make_async_copy(core.at[c, pl.ds(k * each, each)], place_out, core_recv).start()

        @pl.when(v != g)
        def _():
            send(k)

    @pl.loop(0, chunks)
    def _(c):
        wait_bytes(cols.at[c, pl.ds(0, (nk - 1) * ni)], cols_send.at[c])

    wait_bytes(rows_in.at[pl.ds(0, nk - 1)], send_sem.at[0])
    wait_bytes(near_in.at[pl.ds(0, ZL - 1)], send_sem.at[1])
    wait_bytes(far_in.at[pl.ds(0, nh - 1)], send_sem.at[2])
    wait_bytes(total.at[pl.ds(0, nk - 1)], send_sem.at[3])

    wait_bytes(out, core_recv)

    @pl.when(x + side == 0)
    def _():
        wait_bytes(core.at[pl.ds(0, chunks - 1)], core_send)
        wait_bytes(core.at[chunks - 1, pl.ds(0, rank - each)], core_send)

    @pl.when(x + side != 0)
    def _():
        wait_bytes(core, core_send)


def local(nz, nk, field, start):
    nv, ni, na, nb = field.shape
    n1, rank = start.shape
    chunks = 2
    rows = na * nb * nv // (128 * nk * chunks)
    f32 = jnp.float32
    core, basis = pl.pallas_call(
        functools.partial(kernel, nz, nk, nv * na * nz * nb),
        out_shape=(
            jax.ShapeDtypeStruct((nv // nz, rank // nk, na * nz, nb), f32),
            jax.ShapeDtypeStruct((rank, n1), f32),
        ),
        in_specs=[ANY, VMEM],
        out_specs=(ANY, VMEM),
        scratch_shapes=[
            pltpu.VMEM((chunks, n1, rows, 128), f32),
            pltpu.VMEM((chunks, rank, rows, 128), f32),
            pltpu.VMEM((n1, n1), f32),
            pltpu.VMEM((n1, n1), f32),
            pltpu.VMEM((nk, 8, n1), f32),
            pltpu.VMEM((8, n1), f32),
            pltpu.VMEM((ZL, 8, n1), f32),
            pltpu.VMEM((8, n1), f32),
            pltpu.VMEM((nz // ZL, 8, n1), f32),
            pltpu.VMEM((nk, 8, n1), f32),
            pltpu.VMEM((n1, 128), f32),
            pltpu.SemaphoreType.DMA((chunks,)),
            pltpu.SemaphoreType.DMA((chunks,)),
            pltpu.SemaphoreType.DMA((4,)),
            pltpu.SemaphoreType.DMA((4,)),
            pltpu.SemaphoreType.DMA,
            pltpu.SemaphoreType.DMA,
        ],
        compiler_params=pltpu.CompilerParams(
            collective_id=0, has_side_effects=True, vmem_limit_bytes=60 * 2**20
        ),
        name="whole_step",
    )(field, start.T)
    return (core, basis.T)


def solution(mesh):
    placed = (P(None, "blk", "grp", None), P())
    return jax.shard_map(
        functools.partial(local, mesh.shape["grp"], mesh.shape["blk"]),
        mesh=mesh,
        in_specs=placed,
        out_specs=(P("grp", "blk", None, None), P()),
        check_vma=False,
    )
```

time: 711 us -> 166 us (0.23)
  waiting for transfers between devices: 455 us -> 0 us
  Pallas kernels: 0 us -> 162 us
  blocking collectives: 138 us -> 0 us
  other arithmetic: 72.6 us -> 0 us
  matrix products: 15.9 us -> 0 us
  between operations: 14.3 us -> 0.64 us
    psum x1 -> x0, waiting for transfers between devices: 455 us -> none  [local(): gram = lax.psum(gram_local, ('grp', 'blk'))]
    pallas_call x0 -> x1, Pallas kernels: none -> 162 us  [local(): pl.pallas_call(functools.partial(kernel, nz, nk, nv * na * nz * nb), out_...]
    all_to_all x3 -> x0, blocking collectives: 138 us -> none  [the longest x1 60.6 us: local(): lax.all_to_all(field, 'blk', split_axis=2, concat_axis=1, tiled=True)]
    another operation x30 -> x0, other arithmetic: 72.6 us -> none  [the longest x18 39.1 us: orth_once(): lower = jnp.linalg.cholesky(small)]
    dot_general x11 -> x0, matrix products: 14.3 us -> none  [the longest x1 4.83 us: local(): jnp.einsum('ir,vinm->vrnm', basis, mode_one, precision=lax.Precision.HIGH...]
  transfers between devices with their start and end apart: 1 -> 0, of which waited for: 1 -> 0; matrix products, arithmetic and copies ran while one was open for 0% -> 0% of each run, Pallas kernels for 0% -> 0%
where the time goes in v1:
time: 166 us
  Pallas kernels  162 us (98%)
  local copies, waits for them, and re-layouts  3.74 us (2%)
    pallas_call x1, Pallas kernels, local(): pl.pallas_call(functools.partial(kernel, nz, nk, nv * na * nz * nb), out_...  162 us
    unnamed x2, local copies, waits for them, and re-layouts  3.74 us

profile of v1, /device:TPU:1, one launch (start us, length us, event | category | flops | bytes accessed | tf_op | source)
XLA Modules:
  0.0 166.2 jit_solution(5197024804295242778)
XLA Ops:
  0.6 161.9 %whole_step.1 = (f32[1,2,512,256]{3,2,1,0:T(8,128)}, f32[64,256]{1,0:T(8,128)}) custom-call(f32[16,8,32,256]{3,2,1,0:T(8,128)} %field.1, f32[64,256]{1,0:T(8,128)} %bitcast.2), custom_call_target="tpu_custom_call" | custom-call | tf_op jit(solution)/shard_map/whole_step/pallas_call | solution.py:345
  162.5 2.3 %copy.6 = f32[1,2,512,256]{3,2,1,0:T(8,128)} copy(f32[1,2,512,256]{3,2,1,0:T(8,128)} %get-tuple-element.8) | data formatting | bytes 2097152
  164.8 1.5 copy.7

commit v2 on v1

--- a/solution.py
+++ b/solution.py
@@ -143,10 +143,8 @@
     pl.semaphore_wait(barrier, nk - 1 + ZL - 1 + nh - 1)
 
     def variable(c, x, side):
-        zero = (NX - x) // NX
-        up = x + c * (nz // 2 - 2 * x)
-        down = nz - up + zero * (1 - 2 * c) * (nz // 4) + zero * c * (nz // 2)
-        return (g + up + side * (down - up)) % nz
+        up = 1 + x + c * (nz // 2 - 1 - 2 * x)
+        return (g + nz + up + side * (1 - 2 * up)) % nz
 
     def piece(c, dest):
         y, x, side = place(dest)
@@ -326,12 +324,12 @@
 
     wait_bytes(out, core_recv)
 
-    @pl.when(x + side == 0)
+    @pl.when(x + 1 - side == 0)
     def _():
         wait_bytes(core.at[pl.ds(0, chunks - 1)], core_send)
         wait_bytes(core.at[chunks - 1, pl.ds(0, rank - each)], core_send)
 
-    @pl.when(x + side != 0)
+    @pl.when(x + 1 - side != 0)
     def _():
         wait_bytes(core, core_send)
 

time: 166 us -> 183 us (1.10)
  the two profiles are of different devices: /device:TPU:1 before, /device:TPU:35 now
where the time goes in v2:
time: 183 us; the launch traced here: 182 us
  Pallas kernels  178 us (97%)
  local copies, waits for them, and re-layouts  3.74 us (2%)
    pallas_call x1, Pallas kernels, local(): pl.pallas_call(functools.partial(kernel, nz, nk, nv * na * nz * nb), out_...  178 us
    unnamed x2, local copies, waits for them, and re-layouts  3.74 us

profile of v2, /device:TPU:35, one launch (start us, length us, event | category | flops | bytes accessed | tf_op | source)
XLA Modules:
  0.0 182.5 jit_solution(8054090525520105612)
XLA Ops:
  0.6 178.1 %whole_step.1 = (f32[1,2,512,256]{3,2,1,0:T(8,128)}, f32[64,256]{1,0:T(8,128)}) custom-call(f32[16,8,32,256]{3,2,1,0:T(8,128)} %field.1, f32[64,256]{1,0:T(8,128)} %bitcast.2), custom_call_target="tpu_custom_call" | custom-call | tf_op jit(solution)/shard_map/whole_step/pallas_call | solution.py:343
  178.7 2.3 %copy.6 = f32[1,2,512,256]{3,2,1,0:T(8,128)} copy(f32[1,2,512,256]{3,2,1,0:T(8,128)} %get-tuple-element.8) | data formatting | bytes 2097152
  181.0 1.5 copy.7

commit v3 on v2

--- a/solution.py
+++ b/solution.py
@@ -144,7 +144,7 @@
 
     def variable(c, x, side):
         up = 1 + x + c * (nz // 2 - 1 - 2 * x)
-        return (g + nz + up + side * (1 - 2 * up)) % nz
+        return (g + nz + up - 2 * side * up + side * c * ((NX - x) // NX) * (nz // 2)) % nz
 
     def piece(c, dest):
         y, x, side = place(dest)
@@ -324,12 +324,12 @@
 
     wait_bytes(out, core_recv)
 
-    @pl.when(x + 1 - side == 0)
+    @pl.when(x + NC - 1 - side == 0)
     def _():
         wait_bytes(core.at[pl.ds(0, chunks - 1)], core_send)
         wait_bytes(core.at[chunks - 1, pl.ds(0, rank - each)], core_send)
 
-    @pl.when(x + 1 - side != 0)
+    @pl.when(x + NC - 1 - side != 0)
     def _():
         wait_bytes(core, core_send)
 

time: 183 us -> 171 us (0.934)
  the two profiles are of different devices: /device:TPU:35 before, /device:TPU:1 now
where the time goes in v3:
time: 171 us; the launch traced here: 168 us
  Pallas kernels  163 us (95%)
  local copies, waits for them, and re-layouts  3.74 us (2%)
    pallas_call x1, Pallas kernels, local(): pl.pallas_call(functools.partial(kernel, nz, nk, nv * na * nz * nb), out_...  163 us
    unnamed x2, local copies, waits for them, and re-layouts  3.74 us

profile of v3, /device:TPU:1, one launch (start us, length us, event | category | flops | bytes accessed | tf_op | source)
XLA Modules:
  0.0 167.9 jit_solution(7697507191462739532)
XLA Ops:
  0.6 163.5 %whole_step.1 = (f32[1,2,512,256]{3,2,1,0:T(8,128)}, f32[64,256]{1,0:T(8,128)}) custom-call(f32[16,8,32,256]{3,2,1,0:T(8,128)} %field.1, f32[64,256]{1,0:T(8,128)} %bitcast.2), custom_call_target="tpu_custom_call" | custom-call | tf_op jit(solution)/shard_map/whole_step/pallas_call | solution.py:343
  164.1 2.3 %copy.6 = f32[1,2,512,256]{3,2,1,0:T(8,128)} copy(f32[1,2,512,256]{3,2,1,0:T(8,128)} %get-tuple-element.8) | data formatting | bytes 2097152
  166.4 1.5 copy.7

commit v4 on v1

--- a/solution.py
+++ b/solution.py
@@ -31,14 +31,19 @@
     pltpu.make_async_copy(ref, ref, sem).wait()
 
 
-def take(ref, c, a):
-    parts, blocks, rows = ref.shape[:3]
-    return ref.reshape(parts, blocks * rows, 128)[c, pl.ds(a, blocks, stride=rows), :]
-
-
-def put(ref, c, a, value):
-    parts, blocks, rows = ref.shape[:3]
-    ref.reshape(parts, blocks * rows, 128)[c, pl.ds(a, blocks, stride=rows), :] = value
+def take(ref, a):
+    blocks, halves, rows, _ = ref.shape
+    flat = ref.reshape(blocks * halves * rows, 128)
+    return jnp.concatenate(
+        [flat[pl.ds(half * rows + a, blocks, stride=halves * rows), :] for half in range(halves)], axis=1
+    )
+
+
+def put(ref, a, value):
+    blocks, halves, rows, _ = ref.shape
+    flat = ref.reshape(blocks * halves * rows, 128)
+    for half in range(halves):
+        flat[pl.ds(half * rows + a, blocks, stride=halves * rows), :] = value[:, 128 * half : 128 * half + 128]
 
 
 def inverse_factor(small, rank):
@@ -86,7 +91,10 @@
     start,
     out,
     basis_out,
+    here,
+    ready,
     cols,
+    tiles,
     core,
     part,
     cross,
@@ -97,6 +105,7 @@
     far_in,
     total,
     held,
+    load_sem,
     cols_send,
     cols_recv,
     send_sem,
@@ -107,7 +116,7 @@
     g, k = lax.axis_index("grp"), lax.axis_index("blk")
     ny = nk // (NX * NC)
     chunks, rank, na = core.shape[0], core.shape[1], core.shape[2]
-    ni, nb = field.shape[1], field.shape[3] // 128
+    ni = field.shape[1]
     each = rank // nk
     y, x, side = place(k)
     zl, zh = g % ZL, g // ZL
@@ -123,6 +132,7 @@
         step = (s - 1 + side * (nk // 2)) % (nk - 1) + 1
         return shifted(k, (step * 13) % nk, ny)
 
+    pltpu.make_async_copy(field, here, load_sem).start()
     barrier = pltpu.get_barrier_semaphore()
 
     def greet(z, blk):
@@ -150,16 +160,24 @@
 
     def piece(c, dest):
         y, x, side = place(dest)
-        a, b = y // nb, y % nb
-        return field.at[
-            variable(c, x, side), :, pl.ds(pl.multiple_of(a * na, na), na), pl.ds(pl.multiple_of(b * 128, 128), 128)
-        ]
+        return ready.at[variable(c, x, side), y]
 
     def slot(c):
         return cols.at[c, pl.ds(k * ni, ni)]
 
+    wait_bytes(here, load_sem)
+
     @pl.loop(0, chunks)
     def _(c):
+        for place_x in range(NX):
+            for place_side in range(NC):
+                v = variable(c, place_x, place_side)
+                for place_y in range(ny):
+                    for half in range(ready.shape[3]):
+                        ready[v, place_y, :, half] = here[
+                            v, :, na * place_y : na * place_y + na, 128 * half : 128 * half + 128
+                        ]
+
         pltpu.make_async_copy(piece(c, k), slot(c), cols_recv.at[c]).start()
 
         @pl.loop(1, nk)
@@ -181,9 +199,9 @@
     def _(c):
         wait_bytes(cols.at[c], cols_recv.at[c])
 
-        @pl.loop(0, na // 2)
-        def _(p):
-            high, low = split(jnp.concatenate([take(cols, c, 2 * p), take(cols, c, 2 * p + 1)], axis=1))
+        @pl.loop(0, na)
+        def _(a):
+            high, low = split(take(cols.at[c], a))
             part[...] += product(high, high, ((1,), (1,))) + product(low, low, ((1,), (1,)))
             cross[...] += product(high, low, ((1,), (1,)))
 
@@ -272,26 +290,20 @@
 
     high, low = split(turned)
     both = jnp.concatenate([high, low], axis=0)
-    place_out = out.at[
-        0,
-        :,
-        pl.ds(pl.multiple_of((g * (ny // nb) + y // nb) * na, na), na),
-        pl.ds(pl.multiple_of(y % nb * 128, 128), 128),
-    ]
+    place_out = out.at[0, :, pl.ds(pl.multiple_of((g * ny + y) * na, na), na), :]
 
     @pl.loop(0, chunks)
     def _(c):
         v = variable(c, x, side)
 
-        @pl.loop(0, na // 2)
-        def _(p):
-            block_high, block_low = split(
-                jnp.concatenate([take(cols, c, 2 * p), take(cols, c, 2 * p + 1)], axis=1)
-            )
+        @pl.loop(0, na)
+        def _(a):
+            block_high, block_low = split(take(cols.at[c], a))
             first = product(both, block_high, ((1,), (0,)))
-            result = first[:rank] + (first[rank:] + product(high, block_low, ((1,), (0,))))
-            for h in range(2):
-                put(core, c, 2 * p + h, result[:, 128 * h : 128 * h + 128])
+            put(tiles, a, first[:rank] + (first[rank:] + product(high, block_low, ((1,), (0,)))))
+
+        for half in range(tiles.shape[1]):
+            core[c, :, :, 128 * half : 128 * half + 128] = tiles[:, half]
 
         def send(dest):
             pltpu.make_async_remote_copy(
@@ -337,10 +349,11 @@
 
 
 def local(nz, nk, field, start):
-    nv, ni, na, nb = field.shape
+    nv, _, na, nb = field.shape
     n1, rank = start.shape
     chunks = 2
-    rows = na * nb * nv // (128 * nk * chunks)
+    ny = nk // (NX * NC)
+    rows = na // ny
     f32 = jnp.float32
     core, basis = pl.pallas_call(
         functools.partial(kernel, nz, nk, nv * na * nz * nb),
@@ -351,8 +364,11 @@
         in_specs=[ANY, VMEM],
         out_specs=(ANY, VMEM),
         scratch_shapes=[
-            pltpu.VMEM((chunks, n1, rows, 128), f32),
-            pltpu.VMEM((chunks, rank, rows, 128), f32),
+            pltpu.VMEM(field.shape, f32),
+            pltpu.VMEM((nv, ny, field.shape[1], nb // 128, rows, 128), f32),
+            pltpu.VMEM((chunks, n1, nb // 128, rows, 128), f32),
+            pltpu.VMEM((rank, nb // 128, rows, 128), f32),
+            pltpu.VMEM((chunks, rank, rows, nb), f32),
             pltpu.VMEM((n1, n1), f32),
             pltpu.VMEM((n1, n1), f32),
             pltpu.VMEM((nk, 8, n1), f32),
@@ -362,6 +378,7 @@
             pltpu.VMEM((nz // ZL, 8, n1), f32),
             pltpu.VMEM((nk, 8, n1), f32),
             pltpu.VMEM((n1, 128), f32),
+            pltpu.SemaphoreType.DMA,
             pltpu.SemaphoreType.DMA((chunks,)),
             pltpu.SemaphoreType.DMA((chunks,)),
             pltpu.SemaphoreType.DMA((4,)),

time: 166 us -> 167 us (level)
  no operation moved by 1% of the time
where the time goes in v4:
time: 167 us; the launch traced here: 166 us
  Pallas kernels  162 us (97%)
  local copies, waits for them, and re-layouts  3.74 us (2%)
    pallas_call x1, Pallas kernels, local(): pl.pallas_call(functools.partial(kernel, nz, nk, nv * na * nz * nb), out_...  162 us
    unnamed x2, local copies, waits for them, and re-layouts  3.74 us

profile of v4, /device:TPU:1, one launch (start us, length us, event | category | flops | bytes accessed | tf_op | source)
XLA Modules:
  0.0 166.5 jit_solution(490255682647174186)
XLA Ops:
  0.6 162.1 %whole_step.1 = (f32[1,2,512,256]{3,2,1,0:T(8,128)}, f32[64,256]{1,0:T(8,128)}) custom-call(f32[16,8,32,256]{3,2,1,0:T(8,128)} %field.1, f32[64,256]{1,0:T(8,128)} %bitcast.2), custom_call_target="tpu_custom_call" | custom-call | tf_op jit(solution)/shard_map/whole_step/pallas_call | solution.py:358
  162.7 2.3 %copy.6 = f32[1,2,512,256]{3,2,1,0:T(8,128)} copy(f32[1,2,512,256]{3,2,1,0:T(8,128)} %get-tuple-element.8) | data formatting | bytes 2097152
  165.0 1.5 copy.7

commit v5 on v4

--- a/solution.py
+++ b/solution.py
@@ -15,6 +15,23 @@
 NX = 4
 NC = 2
 ZL = 4
+ORDER = (
+    ((1, 1), (-1, -1)),
+    ((-1, -1), (1, 1)),
+    ((1, -1), (-1, 1)),
+    ((-1, 1), (1, -1)),
+    ((2, 1), (-1, 2)),
+    ((2, -1), (1, 2)),
+    ((1, 2), (2, -1)),
+    ((-1, 2), (2, 1)),
+    ((2, 2), (2, 2)),
+    ((2, 0), (0, 2)),
+    ((0, 2), (2, 0)),
+    ((1, 0), (-1, 0)),
+    ((0, 1), (0, -1)),
+    ((-1, 0), (1, 0)),
+    ((0, -1), (0, 1)),
+)
 
 
 def place(k):
@@ -162,6 +179,17 @@
         y, x, side = place(dest)
         return ready.at[variable(c, x, side), y]
 
+    chips = [
+        (
+            (y + (ny + dy) + side * (dy1 - dy)) % ny,
+            (x + (NX + dx) + side * (dx1 - dx)) % NX,
+        )
+        for (dx, dy), (dx1, dy1) in ORDER
+    ]
+    listed = [k + 1 - 2 * side] + [
+        (to_y * NX + to_x) * NC + (side + dcore) % NC for dcore in (1, 0) for to_y, to_x in chips
+    ]
+
     def slot(c):
         return cols.at[c, pl.ds(k * ni, ni)]
 
@@ -180,9 +208,7 @@
 
         pltpu.make_async_copy(piece(c, k), slot(c), cols_recv.at[c]).start()
 
-        @pl.loop(1, nk)
-        def _(s):
-            dest = other(s)
+        for dest in listed:
             pltpu.make_async_remote_copy(
                 src_ref=piece(c, dest),
                 dst_ref=slot(c),

time: 167 us -> 166 us (level)
  no operation moved by 1% of the time
where the time goes in v5:
time: 166 us
  Pallas kernels  161 us (97%)
  local copies, waits for them, and re-layouts  3.74 us (2%)
    pallas_call x1, Pallas kernels, local(): pl.pallas_call(functools.partial(kernel, nz, nk, nv * na * nz * nb), out_...  161 us
    unnamed x2, local copies, waits for them, and re-layouts  3.74 us

profile of v5, /device:TPU:1, one launch (start us, length us, event | category | flops | bytes accessed | tf_op | source)
XLA Modules:
  0.0 165.5 jit_solution(15872438653883523287)
XLA Ops:
  0.6 161.2 %whole_step.1 = (f32[1,2,512,256]{3,2,1,0:T(8,128)}, f32[64,256]{1,0:T(8,128)}) custom-call(f32[16,8,32,256]{3,2,1,0:T(8,128)} %field.1, f32[64,256]{1,0:T(8,128)} %bitcast.2), custom_call_target="tpu_custom_call" | custom-call | tf_op jit(solution)/shard_map/whole_step/pallas_call | solution.py:384
  161.8 2.3 %copy.6 = f32[1,2,512,256]{3,2,1,0:T(8,128)} copy(f32[1,2,512,256]{3,2,1,0:T(8,128)} %get-tuple-element.8) | data formatting | bytes 2097152
  164.1 1.5 copy.7

commit v6 on v5

--- a/solution.py
+++ b/solution.py
@@ -36,12 +36,6 @@
 
 def place(k):
     return k // (NX * NC), (k // NC) % NX, k % NC
-
-
-def shifted(k, step, ny):
-    y, x, core = place(k)
-    dy, dx, dcore = place(step)
-    return (((y + dy) % ny) * NX + (x + dx) % NX) * NC + (core + dcore) % NC
 
 
 def wait_bytes(ref, sem):
@@ -145,10 +139,6 @@
     def far(step):
         return ((zh + step) % nh) * ZL + zl
 
-    def other(s):
-        step = (s - 1 + side * (nk // 2)) % (nk - 1) + 1
-        return shifted(k, (step * 13) % nk, ny)
-
     pltpu.make_async_copy(field, here, load_sem).start()
     barrier = pltpu.get_barrier_semaphore()
 
@@ -157,7 +147,7 @@
 
     @pl.loop(1, nk)
     def _(s):
-        greet(g, other(s))
+        greet(g, (k + s) % nk)
 
     @pl.loop(1, ZL)
     def _(s):
@@ -225,7 +215,7 @@
     def _(c):
         wait_bytes(cols.at[c], cols_recv.at[c])
 
-        @pl.loop(0, na)
+        @pl.loop(0, na, unroll=4)
         def _(a):
             high, low = split(take(cols.at[c], a))
             part[...] += product(high, high, ((1,), (1,))) + product(low, low, ((1,), (1,)))
@@ -236,9 +226,7 @@
     own = pl.ds(pl.multiple_of(k * 8, 8), 8)
     rows_in[k] = part[own, :]
 
-    @pl.loop(1, nk)
-    def _(s):
-        dest = other(s)
+    for dest in listed:
         pltpu.make_async_remote_copy(
             src_ref=part.at[pl.ds(pl.multiple_of(dest * 8, 8), 8)],
             dst_ref=rows_in.at[k],
@@ -281,14 +269,13 @@
     wait_bytes(far_in.at[pl.ds(0, nh - 1)], recv_sem.at[2])
     total[k] = jnp.sum(far_in[...], axis=0) * (1.0 / count)
 
-    @pl.loop(1, nk)
-    def _(s):
+    for dest in listed:
         pltpu.make_async_remote_copy(
             src_ref=total.at[k],
             dst_ref=total.at[k],
             send_sem=send_sem.at[3],
             recv_sem=recv_sem.at[3],
-            device_id=(g, other(s)),
+            device_id=(g, dest),
             device_id_type=MESH,
         ).start()
 
@@ -322,7 +309,7 @@
     def _(c):
         v = variable(c, x, side)
 
-        @pl.loop(0, na)
+        @pl.loop(0, na, unroll=4)
         def _(a):
             block_high, block_low = split(take(cols.at[c], a))
             first = product(both, block_high, ((1,), (0,)))
@@ -341,9 +328,8 @@
                 device_id_type=MESH,
             ).start()
 
-        @pl.loop(1, nk)
-        def _(s):
-            send(other(s))
+        for dest in listed:
+            send(dest)
 
         @pl.when(v == g)
         def _():
@@ -413,7 +399,7 @@
             pltpu.SemaphoreType.DMA,
         ],
         compiler_params=pltpu.CompilerParams(
-            collective_id=0, has_side_effects=True, vmem_limit_bytes=60 * 2**20
+            collective_id=0, has_side_effects=True, vmem_limit_bytes=50 * 2**20
         ),
         name="whole_step",
     )(field, start.T)

time: 166 us -> 159 us (0.958)
  Pallas kernels: 161 us -> 155 us
    pallas_call x1, Pallas kernels: 161 us -> 155 us  [local(): pl.pallas_call(functools.partial(kernel, nz, nk, nv * na * nz * nb), out_...]
    unnamed x2 -> x4, local copies, waits for them, and re-layouts: 3.74 us -> 2.43 us
where the time goes in v6:
time: 159 us; the launch traced here: 158 us
  Pallas kernels  155 us (97%)
  local copies, waits for them, and re-layouts  2.43 us (2%)
    pallas_call x1, Pallas kernels, local(): pl.pallas_call(functools.partial(kernel, nz, nk, nv * na * nz * nb), out_...  155 us

profile of v6, /device:TPU:1, one launch (start us, length us, event | category | flops | bytes accessed | tf_op | source)
XLA Modules:
  0.0 157.9 jit_solution(2992074038708448601)
XLA Ops:
  0.6 0.0 copy-start
  0.6 0.8 copy-done
  1.5 154.8 %whole_step.1 = (f32[1,2,512,256]{3,2,1,0:T(8,128)S(1)}, f32[64,256]{1,0:T(8,128)S(1)}) custom-call(f32[16,8,32,256]{3,2,1,0:T(8,128)} %field.1, f32[64,256]{1,0:T(8,128)S(1)} %bitcast.2), custom_call_target="tpu_custom_call" | custom-call | tf_op jit(solution)/shard_map/whole_step/pallas_call | solution.py:370
  156.3 1.0 copy.6
  157.3 0.6 copy.7
Async XLA Ops:
  0.6 0.8 copy-start
